TPU v7x, 32 devices: a whole 2x2x4 slice. The times are simulated.
32 devices in a mesh: chaos: 8 (over z, y), mesh: 4 (over x, core).
Axes of the slice: x: 2, y: 2, z: 4, core: 2. Of those that a mesh axis runs over, the one named last changes fastest.
Arguments:
- coefficients: bfloat16 [128, 96, 320], P('mesh', None, 'chaos'), may hold values from -6 to 6
- stiffness: bfloat16 [11, 12288, 6, 96], P(None, ('mesh', 'chaos')), may hold values from -0.25 to 0.25
- columns: int32 [128, 6], P('mesh'), may hold values from 0 to 127
- pair_rows: int32 [11, 1280], replicated, may hold values from 0 to 319
- pair_cols: int32 [11, 1280], replicated, may hold values from 0 to 319
- pair_vals: float32 [11, 1280], replicated, may hold values from -2 to 2
Outputs:
- applied: bfloat16 [128, 96, 320], P('mesh', None, 'chaos')
All inputs are finite; a program needn't handle non-finite values.
Results may differ from a plain program's by a relative error of at most 0.001.
Values may be sent and summed in bfloat16 or wider, within the bound.
A program may use at most 320 MiB of HBM per device.

v0:
```python
import jax
import jax.numpy as jnp
from jax import lax
from jax.sharding import PartitionSpec as P


def indicator(indices, count):
    targets = lax.iota(jnp.int32, count)
    return (indices[:, :, None] == targets[None, None, :]).astype(jnp.float32)


def local(coefficients, stiffness, columns, pair_rows, pair_cols, pair_vals):
    whole_nodes = lax.all_gather(coefficients, "mesh", axis=0, tiled=True)
    own_count = coefficients.shape[2]
    node_count = coefficients.shape[0]
    block_size = coefficients.shape[1]
    chaos_count = lax.axis_size("chaos")
    total_count = own_count * chaos_count
    row_count = stiffness.shape[1]
    row_first = lax.axis_index("chaos") * row_count
    row_nodes = (row_first + lax.iota(jnp.int32, row_count)) // block_size
    span = (row_count - 1) // block_size + 2
    peer_first = lax.iota(jnp.int32, chaos_count) * row_count // block_size
    peer_nodes = jnp.minimum(
        peer_first[:, None] + lax.iota(jnp.int32, span)[None, :], node_count - 1
    )
    outgoing = whole_nodes[columns[peer_nodes.reshape(-1)]]
    received = lax.all_to_all(outgoing, "chaos", split_axis=0, concat_axis=3, tiled=True)
    local_index = row_nodes - row_first // block_size
    picked = received[local_index]
    products = jnp.einsum("krsb,rsbj->krj", stiffness, picked, preferred_element_type=jnp.float32)
    weighted = indicator(pair_cols, total_count) * pair_vals[:, :, None]
    every_row = indicator(pair_rows, total_count)
    coupling = jnp.einsum("klj,kli->kji", weighted, every_row, precision=lax.Precision.HIGHEST)
    finished = jnp.einsum(
        "krj,kji->ri", products, coupling, precision=lax.Precision.HIGHEST
    ).astype(jnp.bfloat16)
    returned = lax.all_to_all(finished, "chaos", split_axis=1, concat_axis=0, tiled=True)
    return returned.reshape(node_count, block_size, own_count)


def solution(mesh):
    return jax.shard_map(
        local,
        mesh=mesh,
        in_specs=(
            P("mesh", None, "chaos"),
            P(None, ("mesh", "chaos"), None, None),
            P("mesh", None),
            P(),
            P(),
            P(),
        ),
        out_specs=P("mesh", None, "chaos"),
        check_vma=False,
    )
```

profile of v0, /device:TPU:0, one launch (start us, length us, event | category | flops | bytes accessed | tf_op | source)
XLA Modules:
  0.0 243.4 jit_solution(3743609086238661585)
XLA Ops:
  0.0 13.1 %all_gather.3 = bf16[128,96,40]{1,2,0:T(8,128)(2,1)S(1)} all-gather(bf16[32,96,40]{1,2,0:T(8,128)(2,1)} %param.6), channel_id=1, replica_groups=mesh['chaos'=8,'mesh'=4] {'mesh'}, dimensions={0}, use_global_device_ids=true | all-gather | bytes 1228800 | tf_op jit(solution)/shard_map/all_gather | solution.py:13
  13.1 0.8 copy.19
  13.9 0.1 add_minimum_fusion
  14.0 0.1 min.19
  14.1 0.6 gather_fusion
  14.7 0.1 reshape.124
  14.8 2.5 %gather_fusion.1 = bf16[240,96,40]{1,2,0:T(8,128)(2,1)} fusion(bf16[128,96,40]{1,2,0:T(8,128)(2,1)S(1)} %all_gather.3, s32[1024]{0:T(1024)S(1)} %pad_clamp_fusion.1), kind=kCustom, calls=%fused_computation.1 | custom fusion | bytes 3687360 | tf_op jit(solution)/shard_map/gather | solution.py:27
  17.2 0.0 copy-start.1
  17.2 0.0 copy-start.2
  17.2 0.0 copy-start.3
  17.2 6.0 %all-to-all-start = ((bf16[40,6,96,40]{2,3,1,0:T(8,128)(2,1)}), bf16[40,6,96,40]{2,3,1,0:T(8,128)(2,1)S(1)}, u32[]{:S(2)}, u32[]{:S(2)}) async-start(bf16[40,6,96,40]{2,3,1,0:T(8,128)(2,1)} %bitcast.28), calls=%async_computation | async-start | bytes 4915200 | tf_op jit(solution)/shard_map/all_to_all | solution.py:28
  23.2 12.4 %copy.22 = bf16[11,384,6,96]{3,0,2,1:T(8,128)(2,1)} copy(bf16[11,384,6,96]{1,3,2,0:T(8,128)(2,1)} %param.7) | data formatting | bytes 9732096 | tf_op args[1]
  35.6 0.0 copy-done.1
  35.6 0.0 copy-done.2
  35.6 0.0 copy-done.3
  35.6 42.7 %fusion = f32[11,320,320]{1,2,0:T(8,128)} fusion(s32[11,1280]{1,0:T(8,128)S(1)} %copy-done.1, f32[11,1280]{1,0:T(8,128)S(1)} %copy-done.2, s32[11,1280]{1,0:T(8,128)S(1)} %copy-done.3), kind=kOutput, calls=%fused_computation.4 | convolution fusion | flops 17315020800 | bytes 4674560 | tf_op jit(solution)/shard_map/klj,kli->kji/dot_general | solution.py:34
  78.4 1.3 all-to-all-done
  79.7 0.0 copy-start
  79.7 1.4 copy-done
  81.1 2.4 copy.20
  83.5 62.5 %gather_fusion.2 = bf16[384,6,96,320]{2,3,1,0:T(8,128)(2,1)} fusion(bf16[5,6,96,320]{2,3,1,0:T(8,128)(2,1)S(1)} %bitcast.27, s32[1024]{0:T(1024)S(1)} %pad_clamp_fusion), kind=kCustom, calls=%fused_computation.2 | custom fusion | bytes 283117056 | tf_op jit(solution)/shard_map/gather | solution.py:30
  146.0 68.7 %convolution_bitcast_fusion = f32[11,384,320]{2,0,1:T(8,128)} fusion(bf16[384,6,96,320]{2,3,1,0:T(8,128)(2,1)} %gather_fusion.2, bf16[11,384,6,96]{3,0,2,1:T(8,128)(2,1)} %copy.22), kind=kOutput, calls=%fused_computation.13 | convolution fusion | flops 1557135360 | bytes 151830528 | tf_op jit(solution)/shard_map/krsb,rsbj->krj/dot_general | solution.py:31
  214.7 14.6 %fusion.11 = bf16[384,320]{0,1:T(8,128)(2,1)S(1)} fusion(f32[11,320,320]{1,2,0:T(8,128)} %fusion, f32[11,384,320]{2,0,1:T(8,128)} %convolution_bitcast_fusion), kind=kOutput, calls=%fused_computation.15 | convolution fusion | flops 5190574080 | bytes 10158080 | tf_op jit(solution)/shard_map/krj,kji->ri/dot_general | solution.py:35
  229.2 13.1 %all_to_all.34 = bf16[384,8,40]{0,2,1:T(8,128)(2,1)S(1)} all-to-all(bf16[384,8,40]{0,2,1:T(8,128)(2,1)S(1)} %bitcast.30), channel_id=1, replica_groups=mesh['chaos'=8,'mesh'=4] {'chaos'}, dimensions={1} | all-to-all | bytes 491520 | tf_op jit(solution)/shard_map/all_to_all | solution.py:38
  242.4 0.2 reshape.113
  242.6 0.9 copy.26
  (8 shorter events, 0.1 us)
Async XLA Ops:
  17.2 18.4 %copy-start.1 = (s32[11,1280]{1,0:T(8,128)S(1)}, s32[11,1280]{1,0:T(8,128)}, u32[]{:S(2)}) copy-start(s32[11,1280]{1,0:T(8,128)} %param.9) | copy-start | bytes 168964
  17.2 18.4 %copy-start.2 = (f32[11,1280]{1,0:T(8,128)S(1)}, f32[11,1280]{1,0:T(8,128)}, u32[]{:S(2)}) copy-start(f32[11,1280]{1,0:T(8,128)} %param.11) | copy-start | bytes 168964
  17.2 18.4 %copy-start.3 = (s32[11,1280]{1,0:T(8,128)S(1)}, s32[11,1280]{1,0:T(8,128)}, u32[]{:S(2)}) copy-start(s32[11,1280]{1,0:T(8,128)} %param.10) | copy-start | bytes 168964
  17.2 62.4 %all-to-all-start = ((bf16[40,6,96,40]{2,3,1,0:T(8,128)(2,1)}), bf16[40,6,96,40]{2,3,1,0:T(8,128)(2,1)S(1)}, u32[]{:S(2)}, u32[]{:S(2)}) async-start(bf16[40,6,96,40]{2,3,1,0:T(8,128)(2,1)} %bitcast.28), calls=%async_computation | async-start | bytes 4915200 | tf_op jit(solution)/shard_map/all_to_all | solution.py:28
  79.7 1.4 copy-start
where the time goes:
time: 244 us; the launch traced here: 243 us
  matrix products  126 us (52%)
  local copies, waits for them, and re-layouts  83.7 us (34%)
  blocking collectives  26.2 us (11%)
  starting transfers between devices  5.97 us (2%)
    dot_general x1, matrix products, local(): jnp.einsum('krsb,rsbj->krj', stiffness, picked, preferred_element_type=jn...  68.7 us
    gather x1, local copies, waits for them, and re-layouts, local(): picked = received[local_index]  62.5 us
    dot_general x1, matrix products, local(): jnp.einsum('klj,kli->kji', weighted, every_row, precision=lax.Precision.H...  42.7 us
    dot_general x1, matrix products, local(): jnp.einsum('krj,kji->ri', products, coupling, precision=lax.Precision.HIG...  14.6 us
    unnamed x10, local copies, waits for them, and re-layouts  14.5 us
    all_gather x1, blocking collectives, local(): whole_nodes = lax.all_gather(coefficients, 'mesh', axis=0, tiled=True)  13.1 us
    all_to_all x1, blocking collectives, local(): lax.all_to_all(finished, 'chaos', split_axis=1, concat_axis=0, tiled=True)  13.1 us
    all_to_all x1, starting transfers between devices, local(): lax.all_to_all(outgoing, 'chaos', split_axis=0, concat_axis=3, tiled=True)  5.97 us
  transfers between devices with their start and end apart: 1, of which 1 were waited for; matrix products, arithmetic and copies ran while one was open for 23% of the time, Pallas kernels for 0%

commit v1 on v0

v1 whole, which is shorter than its diff:
```python
import functools

import jax
import jax.numpy as jnp
from jax import lax
from jax.experimental import pallas as pl
from jax.experimental.pallas import tpu as pltpu
from jax.sharding import PartitionSpec as P

LANES = 128
VMEM_BYTES = 56 * 1024 * 1024


def split(value):
    high = value.astype(jnp.bfloat16)
    low = (value - high.astype(jnp.float32)).astype(jnp.bfloat16)
    return high, low


def coupling_kernel(rows_ref, cols_ref, vals_ref, high_ref, low_ref):
    total, pairs = high_ref.shape[1], rows_ref.shape[2]
    targets = lax.broadcasted_iota(jnp.int32, (total, pairs), 0)
    every_row = jnp.where(targets == rows_ref[0], 1.0, 0.0).astype(jnp.bfloat16)
    hit = targets == cols_ref[0]
    value_high, value_low = split(vals_ref[0])
    contract = (((1,), (1,)), ((), ()))
    result = jnp.zeros((total, total), jnp.float32)
    for part in (value_high, value_low):
        weighted = jnp.where(hit, part.astype(jnp.float32), 0.0).astype(jnp.bfloat16)
        result += lax.dot_general(
            every_row, weighted, contract, preferred_element_type=jnp.float32
        )
    high_ref[0], low_ref[0] = split(result)


def coupling_of(pair_rows, pair_cols, pair_vals, total):
    modes, pairs = pair_rows.shape
    entry = pl.BlockSpec((1, 1, pairs), lambda k: (k, 0, 0))
    matrix = pl.BlockSpec((1, total, total), lambda k: (k, 0, 0))
    high, low = pl.pallas_call(
        coupling_kernel,
        grid=(modes,),
        in_specs=[entry] * 3,
        out_specs=[matrix] * 2,
        out_shape=[jax.ShapeDtypeStruct((modes, total, total), jnp.bfloat16)] * 2,
        compiler_params=pltpu.CompilerParams(vmem_limit_bytes=VMEM_BYTES),
        cost_estimate=pl.CostEstimate(
            flops=4 * modes * pairs * total * total,
            bytes_accessed=4 * modes * total * total,
            transcendentals=0,
        ),
    )(pair_rows[:, None], pair_cols[:, None], pair_vals[:, None])
    both = jnp.stack([high, low])
    return both.transpose(0, 2, 1, 3).reshape(2 * total, modes * total)


def spread_kernel(stiff_ref, out_ref):
    _, nnz, block, _ = stiff_ref.shape
    nodes = out_ref.shape[0]
    width = stiff_ref.shape[3] // nodes
    out_ref[...] = jnp.zeros_like(out_ref)
    for s in range(nnz):
        slab = stiff_ref[0, s]
        for n in range(nodes):
            out_ref[n, s * LANES : s * LANES + block, :width] = slab[
                :, n * width : (n + 1) * width
            ]


def spread(stiff, nodes):
    modes, nnz, block, rows = stiff.shape
    return pl.pallas_call(
        spread_kernel,
        grid=(modes,),
        in_specs=[pl.BlockSpec((1, nnz, block, rows), lambda k: (k, 0, 0, 0))],
        out_specs=pl.BlockSpec((nodes, nnz * LANES, LANES), lambda k: (0, 0, k)),
        out_shape=jax.ShapeDtypeStruct(
            (nodes, nnz * LANES, modes * LANES), jnp.bfloat16
        ),
        compiler_params=pltpu.CompilerParams(vmem_limit_bytes=VMEM_BYTES),
        cost_estimate=pl.CostEstimate(
            flops=0, bytes_accessed=8 * modes * nnz * block * rows, transcendentals=0
        ),
    )(stiff)


def pick_kernel(wanted_ref, whole_ref, out_ref):
    @pl.loop(0, out_ref.shape[0])
    def _(at):
        out_ref[at] = whole_ref[wanted_ref[at]]


def pick(wanted, whole):
    return pl.pallas_call(
        pick_kernel,
        in_specs=[
            pl.BlockSpec(memory_space=pltpu.SMEM),
            pl.BlockSpec(memory_space=pltpu.VMEM),
        ],
        out_specs=pl.BlockSpec(memory_space=pltpu.VMEM),
        out_shape=jax.ShapeDtypeStruct(wanted.shape + whole.shape[1:], whole.dtype),
        compiler_params=pltpu.CompilerParams(vmem_limit_bytes=VMEM_BYTES),
    )(wanted, whole)


def apply_kernel(
    nnz, picked_ref, stiff_ref, coupling_ref, out_ref, gathered, high_ref, low_ref
):
    nodes, total, width = out_ref.shape
    block = picked_ref.shape[2]
    modes = stiff_ref.shape[2] // LANES
    group = high_ref.shape[1] // LANES
    gathered[...] = jnp.zeros_like(gathered)
    for first in range(0, nodes, group):
        for g in range(group):
            n = first + g
            for s in range(nnz):
                gathered[:, s * LANES : s * LANES + block] = picked_ref[n * nnz + s]
            lanes = slice(g * LANES, (g + 1) * LANES)
            for k in range(0, modes, 2):
                count = min(2, modes - k)
                product = jnp.dot(
                    gathered[...],
                    stiff_ref[n, :, k * LANES : (k + count) * LANES],
                    preferred_element_type=jnp.float32,
                )
                high, low = split(product)
                for c in range(count):
                    rows = slice((k + c) * total, (k + c + 1) * total)
                    high_ref[rows, lanes] = high[:, c * LANES : (c + 1) * LANES]
                    low_ref[rows, lanes] = low[:, c * LANES : (c + 1) * LANES]
        wide = jnp.dot(
            coupling_ref[...], high_ref[...], preferred_element_type=jnp.float32
        )
        narrow = jnp.dot(
            coupling_ref[:total], low_ref[...], preferred_element_type=jnp.float32
        )
        done = (wide[:total] + (wide[total:] + narrow)).astype(out_ref.dtype)
        for g in range(group):
            out_ref[first + g] = done[:, g * LANES : g * LANES + width]


def apply(picked, stiff, coupling, nnz, width):
    nodes = stiff.shape[0]
    total = picked.shape[1]
    modes = stiff.shape[2] // LANES
    group = 2 if nodes % 2 == 0 else 1
    return pl.pallas_call(
        functools.partial(apply_kernel, nnz),
        in_specs=[pl.BlockSpec(memory_space=pltpu.VMEM)] * 3,
        out_specs=pl.BlockSpec(memory_space=pltpu.VMEM),
        out_shape=jax.ShapeDtypeStruct((nodes, total, width), jnp.bfloat16),
        scratch_shapes=[
            pltpu.VMEM((total, nnz * LANES), jnp.bfloat16),
            pltpu.VMEM((modes * total, group * LANES), jnp.bfloat16),
            pltpu.VMEM((modes * total, group * LANES), jnp.bfloat16),
        ],
        compiler_params=pltpu.CompilerParams(vmem_limit_bytes=VMEM_BYTES),
        cost_estimate=pl.CostEstimate(
            flops=8 * nodes * LANES * modes * total * total,
            bytes_accessed=2 * (picked.size + stiff.size + coupling.size),
            transcendentals=0,
        ),
    )(picked, stiff, coupling)


def local(coefficients, stiffness, columns, pair_rows, pair_cols, pair_vals):
    node_count, block, own = coefficients.shape
    row_count = stiffness.shape[1]
    nnz = columns.shape[1]
    peers = lax.axis_size("chaos")
    total = own * peers
    assert row_count % block == 0 or block % row_count == 0
    span = max(1, row_count // block)
    width = row_count // span

    whole = lax.all_gather(coefficients.transpose(0, 2, 1), "mesh", axis=0, tiled=True)
    wanted = jnp.repeat(columns, block // width, axis=0).reshape(-1) if width < block else columns.reshape(-1)
    outgoing = pick(wanted, whole).reshape(peers, span * nnz, own, block)
    received = lax.all_to_all(outgoing, "chaos", split_axis=0, concat_axis=0, tiled=True)
    picked = received.transpose(1, 0, 2, 3).reshape(span * nnz, total, block)

    stiff = spread(stiffness.transpose(0, 2, 3, 1), span)
    coupling = coupling_of(pair_rows, pair_cols, pair_vals, total)
    finished = apply(picked, stiff, coupling, nnz, width)

    finished = finished.reshape(span, peers, own, width).transpose(1, 0, 2, 3)
    returned = lax.all_to_all(finished, "chaos", split_axis=0, concat_axis=0, tiled=True)
    if width < block:
        returned = returned.reshape(node_count, block // width, own, width)
        return returned.transpose(0, 1, 3, 2).reshape(node_count, block, own)
    return returned.reshape(node_count, own, block).transpose(0, 2, 1)


def solution(mesh):
    return jax.shard_map(
        local,
        mesh=mesh,
        in_specs=(
            P("mesh", None, "chaos"),
            P(None, ("mesh", "chaos"), None, None),
            P("mesh", None),
            P(),
            P(),
            P(),
        ),
        out_specs=P("mesh", None, "chaos"),
        check_vma=False,
    )
```

time: 244 us -> 109 us (0.45)
  matrix products: 126 us -> 0 us
  local copies, waits for them, and re-layouts: 83.7 us -> 24.8 us
  Pallas kernels: 0 us -> 41.1 us
  blocking collectives: 26.2 us -> 32.8 us
  other arithmetic: 0.15 us -> 3.62 us
    dot_general x3 -> x0, matrix products: 126 us -> none  [the longest x1 68.7 us: local(): jnp.einsum('krsb,rsbj->krj', stiffness, picked, preferred_element_type=jn...]
    gather x3 -> x0, local copies, waits for them, and re-layouts: 65.5 us -> none  [the longest x1 62.5 us: local(): picked = received[local_index]]
    pallas_call x0 -> x4, Pallas kernels: none -> 41.1 us  [the longest x1 13.2 us: coupling_of(): pl.pallas_call(coupling_kernel, grid=(modes,), in_specs=[entry] * 3, out_...]
    reshape x2 -> x4, local copies, waits for them, and re-layouts: 1.06 us -> 19.5 us  [the longest x2 17.8 us: coupling_of(): return both.transpose(0, 2, 1, 3).reshape(2 * total, modes * total)]
    unnamed x10 -> x8, local copies, waits for them, and re-layouts: 14.5 us -> 1.54 us
    transpose x0 -> x1, other arithmetic: none -> 3.62 us  [coupling_of(): return both.transpose(0, 2, 1, 3).reshape(2 * total, modes * total)]
    all_to_all x1, blocking collectives: 13.1 us -> 16.7 us  [local(): lax.all_to_all(finished, 'chaos', split_axis=0, concat_axis=0, tiled=True)]
    all_gather x1, blocking collectives: 13.1 us -> 16.1 us  [local(): lax.all_gather(coefficients.transpose(0, 2, 1), 'mesh', axis=0, tiled=True)]
  transfers between devices with their start and end apart: 1 -> 1, of which waited for: 1 -> 0; matrix products, arithmetic and copies ran while one was open for 23% -> 22% of each run, Pallas kernels for 0% -> 22%
where the time goes in v1:
time: 109 us; the launch traced here: 108 us
  Pallas kernels  41.1 us (38%)
  blocking collectives  32.8 us (30%)
  local copies, waits for them, and re-layouts  24.8 us (23%)
  starting transfers between devices  5.83 us (5%)
  other arithmetic  3.62 us (3%)
    reshape x2, local copies, waits for them, and re-layouts, coupling_of(): return both.transpose(0, 2, 1, 3).reshape(2 * total, modes * total)  17.8 us
    all_to_all x1, blocking collectives, local(): lax.all_to_all(finished, 'chaos', split_axis=0, concat_axis=0, tiled=True)  16.7 us
    all_gather x1, blocking collectives, local(): lax.all_gather(coefficients.transpose(0, 2, 1), 'mesh', axis=0, tiled=True)  16.1 us
    pallas_call x1, Pallas kernels, coupling_of(): pl.pallas_call(coupling_kernel, grid=(modes,), in_specs=[entry] * 3, out_...  13.2 us
    pallas_call x1, Pallas kernels, apply(): pl.pallas_call(functools.partial(apply_kernel, nnz), in_specs=[pl.BlockSp...  12.9 us
    pallas_call x1, Pallas kernels, spread(): pl.pallas_call(spread_kernel, grid=(modes,), in_specs=[pl.BlockSpec((1, n...  11 us
    all_to_all x1, starting transfers between devices, local(): lax.all_to_all(outgoing, 'chaos', split_axis=0, concat_axis=0, tiled=True)  5.83 us
    pallas_call x1, Pallas kernels, pick(): pl.pallas_call(pick_kernel, in_specs=[pl.BlockSpec(memory_space=pltpu.SME...  4.01 us
  transfers between devices with their start and end apart: 1, of which 0 were waited for; matrix products, arithmetic and copies ran while one was open for 22% of the time, Pallas kernels for 22%

profile of v1, /device:TPU:0, one launch (start us, length us, event | category | flops | bytes accessed | tf_op | source)
XLA Modules:
  0.0 108.2 jit_solution(605840629203090614)
XLA Ops:
  0.0 0.0 copy-start
  0.0 0.0 copy-start.1
  0.0 0.0 copy-start.2
  0.0 0.8 copy.15
  0.8 0.7 reshape.18.wanted_ref
  1.5 16.1 %all_gather.3.whole_ref = bf16[128,40,96]{2,1,0:T(8,128)(2,1)} all-gather(bf16[32,40,96]{2,1,0:T(8,128)(2,1)} %bitcast.25), channel_id=1, replica_groups=mesh['chaos'=8,'mesh'=4] {'mesh'}, dimensions={0}, use_global_device_ids=true | all-gather | bytes 1228800 | tf_op jit(solution)/shard_map/all_gather | solution.py:177
  17.6 4.0 %shard_map.64 = bf16[192,40,96]{2,1,0:T(8,128)(2,1)} custom-call(s32[192]{0:T(256)} %reshape.18.wanted_ref, bf16[128,40,96]{2,1,0:T(8,128)(2,1)} %all_gather.3.whole_ref), custom_call_target="tpu_custom_call" | custom-call | tf_op jit(solution)/shard_map/pallas_call | solution.py:94
  21.6 5.8 %all-to-all-start = ((bf16[8,24,40,96]{3,2,1,0:T(8,128)(2,1)}), bf16[8,24,40,96]{3,2,1,0:T(8,128)(2,1)S(1)}, u32[]{:S(2)}, u32[]{:S(2)}) async-start(bf16[8,24,40,96]{3,2,1,0:T(8,128)(2,1)} %bitcast.17), calls=%async_computation | async-start | bytes 3932160 | tf_op jit(solution)/shard_map/all_to_all | solution.py:180
  27.4 0.0 copy-done
  27.4 0.7 broadcast_in_dim.9.rows_ref
  28.1 0.0 copy-done.1
  28.1 0.7 broadcast_in_dim.10.cols_ref
  28.7 0.0 copy-done.2
  28.8 0.7 broadcast_in_dim.11.vals_ref
  29.4 13.2 %shard_map.66 = (bf16[11,320,320]{2,1,0:T(8,128)(2,1)}, bf16[11,320,320]{2,1,0:T(8,128)(2,1)}) custom-call(s32[11,1,1280]{2,1,0:T(1,128)} %broadcast_in_dim.9.rows_ref, s32[11,1,1280]{2,1,0:T(1,128)} %broadcast_in_dim.10.cols_ref, f32[11,1,1280]{2,1,0:T(1,128)} %broadcast_in_dim.11.vals_ref), custom_call_target="tpu_custom_call" | custom-call | flops 5767168000 | bytes 4505600 | tf_op jit(solution)/shard_map/pallas_call | solution.py:40
  42.6 3.6 %maximum_bitcast_fusion = bf16[2,320,11,320]{3,1,2,0:T(8,128)(2,1)S(1)} fusion(bf16[1,11,320,320]{3,2,1,0:T(8,128)(2,1)} %bitcast.20, bf16[1,11,320,320]{3,2,1,0:T(8,128)(2,1)} %bitcast.19), kind=kLoop, calls=%fused_computation | loop fusion | flops 2252800 | bytes 9011200 | tf_op jit(solution)/shard_map/transpose | solution.py:54
  46.2 6.6 %copy.20 = bf16[2,320,11,320]{3,2,1,0:T(8,128)(2,1)} copy(bf16[2,320,11,320]{3,1,2,0:T(8,128)(2,1)S(1)} %maximum_bitcast_fusion) | data formatting | bytes 9011200 | tf_op jit(solution)/shard_map/reshape | solution.py:54
  52.7 11.3 %reshape.24.coupling_ref = bf16[640,3520]{1,0:T(8,128)(2,1)} reshape(bf16[2,320,11,320]{3,2,1,0:T(8,128)(2,1)} %copy.20) | data formatting | bytes 9011200 | tf_op jit(solution)/shard_map/reshape | solution.py:54
  64.0 11.0 %shard_map.65.stiff_ref = bf16[4,768,1408]{2,1,0:T(8,128)(2,1)} custom-call(bf16[11,6,96,384]{3,2,1,0:T(8,128)(2,1)} %bitcast.18), custom_call_target="tpu_custom_call" | custom-call | bytes 19464192 | tf_op jit(solution)/shard_map/pallas_call | solution.py:72
  75.1 0.0 all-to-all-done
  75.1 1.8 %copy.16 = bf16[24,8,40,96]{3,2,1,0:T(8,128)(2,1)} copy(bf16[24,8,40,96]{3,2,0,1:T(8,128)(2,1)S(1)} %bitcast.16) | data formatting | bytes 2949120 | tf_op jit(solution)/shard_map/transpose | solution.py:181
  76.9 12.9 %shard_map.67 = bf16[4,320,96]{2,1,0:T(8,128)(2,1)} custom-call(bf16[24,320,96]{2,1,0:T(8,128)(2,1)} %bitcast.21, bf16[4,768,1408]{2,1,0:T(8,128)(2,1)} %shard_map.65.stiff_ref, bf16[640,3520]{1,0:T(8,128)(2,1)} %reshape.24.coupling_ref), custom_call_target="tpu_custom_call" | custom-call | flops 4613734400 | bytes 14630912 | tf_op jit(solution)/shard_map/pallas_call | solution.py:148
  89.8 1.0 copy.23
  90.8 16.7 %all_to_all.10 = bf16[8,4,40,96]{3,2,1,0:T(8,128)(2,1)S(1)} all-to-all(bf16[8,4,40,96]{3,2,1,0:T(8,128)(2,1)S(1)} %bitcast.22), channel_id=1, replica_groups=mesh['chaos'=8,'mesh'=4] {'chaos'}, dimensions={0} | all-to-all | bytes 491520 | tf_op jit(solution)/shard_map/all_to_all | solution.py:188
  107.5 0.7 copy.25
Async XLA Ops:
  0.0 27.4 %copy-start = (s32[11,1280]{1,0:T(8,128)S(1)}, s32[11,1280]{1,0:T(8,128)}, u32[]{:S(2)}) copy-start(s32[11,1280]{1,0:T(8,128)} %param.9) | copy-start | bytes 168964
  0.0 28.1 %copy-start.1 = (s32[11,1280]{1,0:T(8,128)S(1)}, s32[11,1280]{1,0:T(8,128)}, u32[]{:S(2)}) copy-start(s32[11,1280]{1,0:T(8,128)} %param.10) | copy-start | bytes 168964
  0.0 28.7 %copy-start.2 = (f32[11,1280]{1,0:T(8,128)S(1)}, f32[11,1280]{1,0:T(8,128)}, u32[]{:S(2)}) copy-start(f32[11,1280]{1,0:T(8,128)} %param.11) | copy-start | bytes 168964
  21.6 53.5 %all-to-all-start = ((bf16[8,24,40,96]{3,2,1,0:T(8,128)(2,1)}), bf16[8,24,40,96]{3,2,1,0:T(8,128)(2,1)S(1)}, u32[]{:S(2)}, u32[]{:S(2)}) async-start(bf16[8,24,40,96]{3,2,1,0:T(8,128)(2,1)} %bitcast.17), calls=%async_computation | async-start | bytes 3932160 | tf_op jit(solution)/shard_map/all_to_all | solution.py:180

commit v2 on v0

v2 whole, which is shorter than its diff:
```python
import functools

import jax
import jax.numpy as jnp
from jax import lax
from jax.experimental import pallas as pl
from jax.experimental.pallas import tpu as pltpu
from jax.sharding import PartitionSpec as P

LANES = 128
VMEM_BYTES = 60 * 1024 * 1024
MESH = pl.DeviceIdType.MESH


def split(value):
    high = value.astype(jnp.bfloat16)
    low = (value - high.astype(jnp.float32)).astype(jnp.bfloat16)
    return high, low


def remote(source, target, send, receive, axis, peer):
    return pltpu.make_async_remote_copy(
        src_ref=source,
        dst_ref=target,
        send_sem=send,
        recv_sem=receive,
        device_id={axis: peer},
        device_id_type=MESH,
    )


def kernel(
    peers,
    parts,
    wanted_ref,
    own_ref,
    stiff_hbm,
    rows_ref,
    cols_ref,
    vals_ref,
    out_ref,
    whole,
    outgoing,
    received,
    finished,
    stiff,
    spread,
    coupling,
    wide_pick,
    picked,
    high_ref,
    low_ref,
    stiff_sem,
    part_send,
    part_recv,
    pick_send,
    pick_recv,
    done_send,
    done_recv,
):
    me, part = lax.axis_index("chaos"), lax.axis_index("mesh")
    nodes, own, block = own_ref.shape
    modes, nnz, _, row_count = stiff.shape
    span, width = out_ref.shape[1], out_ref.shape[3]
    total = peers * own
    padded = coupling.shape[1] // modes
    pairs = rows_ref.shape[1]
    group = high_ref.shape[1] // LANES

    barrier = pltpu.get_barrier_semaphore()

    @pl.loop(1, parts)
    def _(step):
        pl.semaphore_signal(barrier, inc=1, device_id={"mesh": lax.rem(part + step, parts)}, device_id_type=MESH)

    @pl.loop(1, peers)
    def _(step):
        pl.semaphore_signal(barrier, inc=1, device_id={"chaos": lax.rem(me + step, peers)}, device_id_type=MESH)

    stiff_copy = pltpu.make_async_copy(stiff_hbm, stiff, stiff_sem)
    stiff_copy.start()
    pl.semaphore_wait(barrier, parts + peers - 2)

    def part_copy(step):
        slot = pl.ds(part * nodes, nodes)
        return remote(own_ref, whole.at[slot], part_send.at[step], part_recv.at[step], "mesh", lax.rem(part + step, parts))

    @pl.loop(1, parts)
    def _(step):
        part_copy(step).start()

    whole[pl.ds(part * nodes, nodes)] = own_ref[...]

    spread[...] = jnp.zeros_like(spread)
    stiff_copy.wait()

    @pl.loop(0, modes)
    def _(k):
        for s in range(nnz):
            slab = stiff[k, s]
            for n in range(span):
                spread[k, n, s * LANES : s * LANES + block, :width] = slab[:, n * width : (n + 1) * width]

    @pl.loop(1, parts)
    def _(step):
        part_copy(step).wait()

    count = span * nnz

    def pick_copy(step):
        peer = lax.rem(me + step, peers)
        return remote(outgoing.at[peer], received.at[me], pick_send.at[step], pick_recv.at[step], "chaos", peer)

    @pl.loop(1, peers)
    def _(step):
        peer = lax.rem(me + step, peers)
        for at in range(count):
            outgoing[peer, at] = whole[wanted_ref[peer * count + at]]
        pick_copy(step).start()

    for at in range(count):
        received[me, at] = whole[wanted_ref[me * count + at]]

    @pl.loop(0, modes)
    def _(k):
        target_row = lax.broadcasted_iota(jnp.int32, (total, pairs), 0)
        target_col = lax.broadcasted_iota(jnp.int32, (padded, pairs), 0)
        at = pl.ds(k, 1)
        every_row = jnp.where(target_row == rows_ref[at], 1.0, 0.0).astype(jnp.bfloat16)
        hit = target_col == cols_ref[at]
        result = jnp.zeros((total, padded), jnp.float32)
        for value in split(vals_ref[at]):
            weighted = jnp.where(hit, value.astype(jnp.float32), 0.0).astype(jnp.bfloat16)
            result += lax.dot_general(
                every_row, weighted, (((1,), (1,)), ((), ())), preferred_element_type=jnp.float32
            )
        lanes = pl.ds(pl.multiple_of(k * padded, LANES), padded)
        coupling[:total, lanes], coupling[total:, lanes] = split(result)

    wide_pick[...] = jnp.zeros_like(wide_pick)
    if padded > total:
        for k in range(modes):
            gap = slice(k * padded + total, (k + 1) * padded)
            high_ref[gap] = jnp.zeros_like(high_ref[gap])
            low_ref[gap] = jnp.zeros_like(low_ref[gap])

    @pl.loop(1, peers)
    def _(step):
        pick_copy(step).wait()

    def done_copy(turn, step):
        peer = lax.rem(me + step, peers)
        slot = pl.ds(turn * group, group)
        return remote(
            finished.at[peer, slot], out_ref.at[me, slot], done_send.at[turn, step], done_recv.at[turn, step], "chaos", peer
        )

    for turn in range(span // group):
        for g in range(group):
            n = turn * group + g
            for s in range(nnz):
                for c in range(peers):
                    wide_pick[c * own : (c + 1) * own, s * LANES : s * LANES + block] = received[c, n * nnz + s].astype(jnp.float32)
            picked[...] = wide_pick[...].astype(jnp.bfloat16)
            lanes = slice(g * LANES, (g + 1) * LANES)
            for k in range(0, modes, 2):
                some = min(2, modes - k)
                weights = jnp.concatenate([spread[k + c, n] for c in range(some)], axis=1)
                high, low = split(jnp.dot(picked[...], weights, preferred_element_type=jnp.float32))
                for c in range(some):
                    rows = slice((k + c) * padded, (k + c) * padded + total)
                    high_ref[rows, lanes] = high[:, c * LANES : (c + 1) * LANES]
                    low_ref[rows, lanes] = low[:, c * LANES : (c + 1) * LANES]
        wide = jnp.dot(coupling[...], high_ref[...], preferred_element_type=jnp.float32)
        narrow = jnp.dot(coupling[:total], low_ref[...], preferred_element_type=jnp.float32)
        done = wide[:total] + (wide[total:] + narrow)
        for g in range(group):
            for c in range(peers):
                finished[c, turn * group + g] = done[c * own : (c + 1) * own, g * LANES : g * LANES + width].astype(jnp.bfloat16)

        @pl.loop(1, peers)
        def _(step):
            done_copy(turn, step).start()

        slot = pl.ds(turn * group, group)
        out_ref[me, slot] = finished[me, slot]

    for turn in range(span // group):

        @pl.loop(1, peers)
        def _(step):
            done_copy(turn, step).wait()


def local(coefficients, stiffness, columns, pair_rows, pair_cols, pair_vals):
    node_count, block, own = coefficients.shape
    modes, row_count, nnz, _ = stiffness.shape
    peers, parts = lax.axis_size("chaos"), lax.axis_size("mesh")
    total = own * peers
    assert row_count % block == 0 or block % row_count == 0
    span = max(1, row_count // block)
    width = row_count // span
    group = 2 if span % 2 == 0 else 1
    padded = -(-total // LANES) * LANES
    wanted = jnp.repeat(columns, block // width, axis=0).reshape(-1)
    bf16 = jnp.bfloat16
    vmem = pl.BlockSpec(memory_space=pltpu.VMEM)
    returned = pl.pallas_call(
        functools.partial(kernel, peers, parts),
        in_specs=[
            pl.BlockSpec(memory_space=pltpu.SMEM),
            vmem,
            pl.BlockSpec(memory_space=pl.ANY),
            vmem,
            vmem,
            vmem,
        ],
        out_specs=vmem,
        out_shape=jax.ShapeDtypeStruct((peers, span, own, width), bf16),
        scratch_shapes=[
            pltpu.VMEM((parts * node_count, own, block), bf16),
            pltpu.VMEM((peers, span * nnz, own, block), bf16),
            pltpu.VMEM((peers, span * nnz, own, block), bf16),
            pltpu.VMEM((peers, span, own, width), bf16),
            pltpu.VMEM((modes, nnz, block, row_count), bf16),
            pltpu.VMEM((modes, span, nnz * LANES, LANES), bf16),
            pltpu.VMEM((2 * total, modes * padded), bf16),
            pltpu.VMEM((total, nnz * LANES), jnp.float32),
            pltpu.VMEM((total, nnz * LANES), bf16),
            pltpu.VMEM((modes * padded, group * LANES), bf16),
            pltpu.VMEM((modes * padded, group * LANES), bf16),
            pltpu.SemaphoreType.DMA,
            pltpu.SemaphoreType.DMA((parts,)),
            pltpu.SemaphoreType.DMA((parts,)),
            pltpu.SemaphoreType.DMA((peers,)),
            pltpu.SemaphoreType.DMA((peers,)),
            pltpu.SemaphoreType.DMA((span // group, peers)),
            pltpu.SemaphoreType.DMA((span // group, peers)),
        ],
        compiler_params=pltpu.CompilerParams(
            collective_id=0, has_side_effects=True, vmem_limit_bytes=VMEM_BYTES
        ),
    )(
        wanted,
        coefficients.transpose(0, 2, 1),
        stiffness.transpose(0, 2, 3, 1),
        pair_rows,
        pair_cols,
        pair_vals,
    )
    if width < block:
        returned = returned.reshape(node_count, block // width, own, width)
        return returned.transpose(0, 1, 3, 2).reshape(node_count, block, own)
    return returned.reshape(node_count, own, block).transpose(0, 2, 1)


def solution(mesh):
    return jax.shard_map(
        local,
        mesh=mesh,
        in_specs=(
            P("mesh", None, "chaos"),
            P(None, ("mesh", "chaos"), None, None),
            P("mesh", None),
            P(),
            P(),
            P(),
        ),
        out_specs=P("mesh", None, "chaos"),
        check_vma=False,
    )
```

time: 244 us -> 88.1 us (0.36)
  matrix products: 126 us -> 0 us
  Pallas kernels: 0 us -> 84.7 us
  local copies, waits for them, and re-layouts: 83.7 us -> 3.16 us
  blocking collectives: 26.2 us -> 0 us
  starting transfers between devices: 5.97 us -> 0 us
    dot_general x3 -> x0, matrix products: 126 us -> none  [the longest x1 68.7 us: local(): jnp.einsum('krsb,rsbj->krj', stiffness, picked, preferred_element_type=jn...]
    pallas_call x0 -> x1, Pallas kernels: none -> 84.7 us  [local(): pl.pallas_call(functools.partial(kernel, peers, parts), in_specs=[pl.Bloc...]
    gather x3 -> x0, local copies, waits for them, and re-layouts: 65.5 us -> none  [the longest x1 62.5 us: local(): picked = received[local_index]]
    all_gather x1 -> x0, blocking collectives: 13.1 us -> none  [local(): whole_nodes = lax.all_gather(coefficients, 'mesh', axis=0, tiled=True)]
    all_to_all x1 -> x0, blocking collectives: 13.1 us -> none  [local(): lax.all_to_all(finished, 'chaos', split_axis=1, concat_axis=0, tiled=True)]
    unnamed x10 -> x2, local copies, waits for them, and re-layouts: 14.5 us -> 2.49 us
    all_to_all x1 -> x0, starting transfers between devices: 5.97 us -> none  [local(): lax.all_to_all(outgoing, 'chaos', split_axis=0, concat_axis=3, tiled=True)]
  transfers between devices with their start and end apart: 1 -> 0, of which waited for: 1 -> 0; matrix products, arithmetic and copies ran while one was open for 23% -> 0% of each run, Pallas kernels for 0% -> 0%
where the time goes in v2:
time: 88.1 us; the launch traced here: 87.9 us
  Pallas kernels  84.7 us (96%)
  local copies, waits for them, and re-layouts  3.16 us (4%)
    pallas_call x1, Pallas kernels, local(): pl.pallas_call(functools.partial(kernel, peers, parts), in_specs=[pl.Bloc...  84.7 us
    unnamed x2, local copies, waits for them, and re-layouts  2.49 us

profile of v2, /device:TPU:0, one launch (start us, length us, event | category | flops | bytes accessed | tf_op | source)
XLA Modules:
  0.0 87.9 jit_solution(15161920728959759988)
XLA Ops:
  0.0 0.8 copy.7
  0.8 0.7 reshape_reshape_broadcast_in_dim.3.wanted_ref
  1.4 84.7 %shard_map.64 = bf16[8,4,40,96]{3,2,1,0:T(8,128)(2,1)} custom-call(s32[192]{0:T(256)} %reshape_reshape_broadcast_in_dim.3.wanted_ref, bf16[32,40,96]{2,1,0:T(8,128)(2,1)} %bitcast.7, bf16[11,6,96,384]{3,2,1,0:T(8,128)(2,1)} %bitcast.5, s32[11,1280]{1,0:T(8,128)} %rows_ref.1, s32[11,1280]{1,0:T(8,128)} %cols_ref.1, f32[11,1280]{1,0:T(8,128)} %vals_ref.1), custom_call_target="tpu_custom_call" | custom-call | tf_op jit(solution)/shard_map/pallas_call | solution.py:208
  86.2 1.7 %copy.9 = bf16[32,96,40]{1,2,0:T(8,128)(2,1)} copy(bf16[32,96,40]{1,2,0:T(8,128)(2,1)} %bitcast.6) | data formatting | bytes 491520

commit v3 on v2

--- a/solution.py
+++ b/solution.py
@@ -39,6 +39,7 @@
     cols_ref,
     vals_ref,
     out_ref,
+    gathered,
     whole,
     outgoing,
     received,
@@ -81,15 +82,26 @@
     stiff_copy.start()
     pl.semaphore_wait(barrier, parts + peers - 2)
 
-    def part_copy(step):
-        slot = pl.ds(part * nodes, nodes)
-        return remote(own_ref, whole.at[slot], part_send.at[step], part_recv.at[step], "mesh", lax.rem(part + step, parts))
-
-    @pl.loop(1, parts)
-    def _(step):
-        part_copy(step).start()
-
-    whole[pl.ds(part * nodes, nodes)] = own_ref[...]
+    pack = gathered.shape[3] // block
+    half = parts // 2
+    partner = part + 1 - 2 * lax.rem(part, 2)
+
+    def part_copy(slot, peer, at):
+        return remote(gathered.at[slot], gathered.at[slot], part_send.at[at], part_recv.at[at], "mesh", peer)
+
+    def same_copy(step):
+        return part_copy(part, lax.rem(part + 2 * step, parts), step)
+
+    def forward_copy(step):
+        return part_copy(lax.rem(part + parts - 2 * step, parts), partner, half + step)
+
+    for n in range(nodes):
+        lanes = slice(n % pack * block, (n % pack + 1) * block)
+        gathered[part, n // pack, :, lanes] = own_ref[n]
+
+    for step in range(1, half):
+        same_copy(step).start()
+    part_copy(part, partner, 0).start()
 
     spread[...] = jnp.zeros_like(spread)
     stiff_copy.wait()
@@ -99,27 +111,42 @@
         for s in range(nnz):
             slab = stiff[k, s]
             for n in range(span):
-                spread[k, n, s * LANES : s * LANES + block, :width] = slab[:, n * width : (n + 1) * width]
-
-    @pl.loop(1, parts)
-    def _(step):
-        part_copy(step).wait()
-
-    count = span * nnz
+                spread[k, n, s * block : (s + 1) * block, :width] = slab[:, n * width : (n + 1) * width]
+
+    for step in range(1, half):
+        same_copy(step).wait()
+        forward_copy(step).start()
+    part_copy(part, partner, 0).wait()
+    for step in range(1, half):
+        forward_copy(step).wait()
+
+    @pl.loop(0, parts)
+    def _(p):
+        for n in range(nodes):
+            lanes = slice(n % pack * block, (n % pack + 1) * block)
+            whole[p * nodes + n] = gathered[p, n // pack, :, lanes]
+
+    share = block // width
+
+    def pick(target, slot, peer):
+        for n in range(span):
+            node = peer * span // share + n
+            for s in range(nnz):
+                at = (n * nnz + s) * block
+                target[slot, :, at : at + block] = whole[wanted_ref[s, node]]
 
     def pick_copy(step):
         peer = lax.rem(me + step, peers)
         return remote(outgoing.at[peer], received.at[me], pick_send.at[step], pick_recv.at[step], "chaos", peer)
 
     @pl.loop(1, peers)
-    def _(step):
+    def _(turn):
+        step = 1 + lax.rem(turn - 2 + peers // 2, peers - 1)
         peer = lax.rem(me + step, peers)
-        for at in range(count):
-            outgoing[peer, at] = whole[wanted_ref[peer * count + at]]
+        pick(outgoing, peer, peer)
         pick_copy(step).start()
 
-    for at in range(count):
-        received[me, at] = whole[wanted_ref[me * count + at]]
+    pick(received, me, me)
 
     @pl.loop(0, modes)
     def _(k):
@@ -137,7 +164,6 @@
         lanes = pl.ds(pl.multiple_of(k * padded, LANES), padded)
         coupling[:total, lanes], coupling[total:, lanes] = split(result)
 
-    wide_pick[...] = jnp.zeros_like(wide_pick)
     if padded > total:
         for k in range(modes):
             gap = slice(k * padded + total, (k + 1) * padded)
@@ -158,9 +184,8 @@
     for turn in range(span // group):
         for g in range(group):
             n = turn * group + g
-            for s in range(nnz):
-                for c in range(peers):
-                    wide_pick[c * own : (c + 1) * own, s * LANES : s * LANES + block] = received[c, n * nnz + s].astype(jnp.float32)
+            for c in range(peers):
+                wide_pick[c * own : (c + 1) * own] = received[c, :, n * nnz * block : (n + 1) * nnz * block].astype(jnp.float32)
             picked[...] = wide_pick[...].astype(jnp.bfloat16)
             lanes = slice(g * LANES, (g + 1) * LANES)
             for k in range(0, modes, 2):
@@ -198,11 +223,12 @@
     peers, parts = lax.axis_size("chaos"), lax.axis_size("mesh")
     total = own * peers
     assert row_count % block == 0 or block % row_count == 0
+    assert parts % 2 == 0
     span = max(1, row_count // block)
     width = row_count // span
     group = 2 if span % 2 == 0 else 1
     padded = -(-total // LANES) * LANES
-    wanted = jnp.repeat(columns, block // width, axis=0).reshape(-1)
+    pack = 4 if node_count % 4 == 0 else 1
     bf16 = jnp.bfloat16
     vmem = pl.BlockSpec(memory_space=pltpu.VMEM)
     returned = pl.pallas_call(
@@ -218,15 +244,16 @@
         out_specs=vmem,
         out_shape=jax.ShapeDtypeStruct((peers, span, own, width), bf16),
         scratch_shapes=[
+            pltpu.VMEM((parts, node_count // pack, own, pack * block), bf16),
             pltpu.VMEM((parts * node_count, own, block), bf16),
-            pltpu.VMEM((peers, span * nnz, own, block), bf16),
-            pltpu.VMEM((peers, span * nnz, own, block), bf16),
+            pltpu.VMEM((peers, own, span * nnz * block), bf16),
+            pltpu.VMEM((peers, own, span * nnz * block), bf16),
             pltpu.VMEM((peers, span, own, width), bf16),
             pltpu.VMEM((modes, nnz, block, row_count), bf16),
-            pltpu.VMEM((modes, span, nnz * LANES, LANES), bf16),
+            pltpu.VMEM((modes, span, nnz * block, LANES), bf16),
             pltpu.VMEM((2 * total, modes * padded), bf16),
-            pltpu.VMEM((total, nnz * LANES), jnp.float32),
-            pltpu.VMEM((total, nnz * LANES), bf16),
+            pltpu.VMEM((total, nnz * block), jnp.float32),
+            pltpu.VMEM((total, nnz * block), bf16),
             pltpu.VMEM((modes * padded, group * LANES), bf16),
             pltpu.VMEM((modes * padded, group * LANES), bf16),
             pltpu.SemaphoreType.DMA,
@@ -241,7 +268,7 @@
             collective_id=0, has_side_effects=True, vmem_limit_bytes=VMEM_BYTES
         ),
     )(
-        wanted,
+        columns.T,
         coefficients.transpose(0, 2, 1),
         stiffness.transpose(0, 2, 3, 1),
         pair_rows,

time: 88.1 us -> 69.6 us (0.79)
  Pallas kernels: 84.7 us -> 67.8 us
  local copies, waits for them, and re-layouts: 3.16 us -> 1.73 us
    pallas_call x1, Pallas kernels: 84.7 us -> 67.8 us  [local(): pl.pallas_call(functools.partial(kernel, peers, parts), in_specs=[pl.Bloc...]
    unnamed x2 -> x1, local copies, waits for them, and re-layouts: 2.49 us -> 1.73 us
where the time goes in v3:
time: 69.6 us; the launch traced here: 69.5 us
  Pallas kernels  67.8 us (97%)
  local copies, waits for them, and re-layouts  1.73 us (2%)
    pallas_call x1, Pallas kernels, local(): pl.pallas_call(functools.partial(kernel, peers, parts), in_specs=[pl.Bloc...  67.8 us
    unnamed x1, local copies, waits for them, and re-layouts  1.73 us

profile of v3, /device:TPU:0, one launch (start us, length us, event | category | flops | bytes accessed | tf_op | source)
XLA Modules:
  0.0 69.5 jit_solution(8490906326997606497)
XLA Ops:
  0.0 67.8 %shard_map.64 = bf16[8,4,40,96]{3,2,1,0:T(8,128)(2,1)} custom-call(s32[6,32]{1,0:T(8,128)} %bitcast.9, bf16[32,40,96]{2,1,0:T(8,128)(2,1)} %bitcast.8, bf16[11,6,96,384]{3,2,1,0:T(8,128)(2,1)} %bitcast.6, s32[11,1280]{1,0:T(8,128)} %rows_ref.1, s32[11,1280]{1,0:T(8,128)} %cols_ref.1, f32[11,1280]{1,0:T(8,128)} %vals_ref.1), custom_call_target="tpu_custom_call" | custom-call | tf_op jit(solution)/shard_map/pallas_call | solution.py:234
  67.8 1.7 %copy.8 = bf16[32,96,40]{1,2,0:T(8,128)(2,1)} copy(bf16[32,96,40]{1,2,0:T(8,128)(2,1)} %bitcast.7) | data formatting | bytes 491520

commit v4 on v3

--- a/solution.py
+++ b/solution.py
@@ -103,6 +103,41 @@
         same_copy(step).start()
     part_copy(part, partner, 0).start()
 
+    for step in range(1, half):
+        same_copy(step).wait()
+        forward_copy(step).start()
+    part_copy(part, partner, 0).wait()
+    for step in range(1, half):
+        forward_copy(step).wait()
+
+    @pl.loop(0, parts)
+    def _(p):
+        for n in range(nodes):
+            lanes = slice(n % pack * block, (n % pack + 1) * block)
+            whole[p * nodes + n] = gathered[p, n // pack, :, lanes]
+
+    share = block // width
+
+    def pick(target, slot, peer):
+        for n in range(span):
+            node = peer * span // share + n
+            for s in range(nnz):
+                at = (n * nnz + s) * block
+                target[slot, :, at : at + block] = whole[wanted_ref[s, node]]
+
+    def pick_copy(step):
+        peer = lax.rem(me + step, peers)
+        return remote(outgoing.at[peer], received.at[me], pick_send.at[step], pick_recv.at[step], "chaos", peer)
+
+    @pl.loop(1, peers)
+    def _(turn):
+        step = 1 + lax.rem(turn - 2 + peers // 2, peers - 1)
+        peer = lax.rem(me + step, peers)
+        pick(outgoing, peer, peer)
+        pick_copy(step).start()
+
+    pick(received, me, me)
+
     spread[...] = jnp.zeros_like(spread)
     stiff_copy.wait()
 
@@ -112,41 +147,6 @@
             slab = stiff[k, s]
             for n in range(span):
                 spread[k, n, s * block : (s + 1) * block, :width] = slab[:, n * width : (n + 1) * width]
-
-    for step in range(1, half):
-        same_copy(step).wait()
-        forward_copy(step).start()
-    part_copy(part, partner, 0).wait()
-    for step in range(1, half):
-        forward_copy(step).wait()
-
-    @pl.loop(0, parts)
-    def _(p):
-        for n in range(nodes):
-            lanes = slice(n % pack * block, (n % pack + 1) * block)
-            whole[p * nodes + n] = gathered[p, n // pack, :, lanes]
-
-    share = block // width
-
-    def pick(target, slot, peer):
-        for n in range(span):
-            node = peer * span // share + n
-            for s in range(nnz):
-                at = (n * nnz + s) * block
-                target[slot, :, at : at + block] = whole[wanted_ref[s, node]]
-
-    def pick_copy(step):
-        peer = lax.rem(me + step, peers)
-        return remote(outgoing.at[peer], received.at[me], pick_send.at[step], pick_recv.at[step], "chaos", peer)
-
-    @pl.loop(1, peers)
-    def _(turn):
-        step = 1 + lax.rem(turn - 2 + peers // 2, peers - 1)
-        peer = lax.rem(me + step, peers)
-        pick(outgoing, peer, peer)
-        pick_copy(step).start()
-
-    pick(received, me, me)
 
     @pl.loop(0, modes)
     def _(k):

time: 69.6 us -> 69.7 us (level)
  no operation moved by 1% of the time
where the time goes in v4:
time: 69.7 us; the launch traced here: 69.5 us
  Pallas kernels  67.8 us (97%)
  local copies, waits for them, and re-layouts  1.73 us (2%)
    pallas_call x1, Pallas kernels, local(): pl.pallas_call(functools.partial(kernel, peers, parts), in_specs=[pl.Bloc...  67.8 us
    unnamed x1, local copies, waits for them, and re-layouts  1.73 us

profile of v4, /device:TPU:0, one launch (start us, length us, event | category | flops | bytes accessed | tf_op | source)
XLA Modules:
  0.0 69.5 jit_solution(13745825823082917098)
XLA Ops:
  0.0 67.8 %shard_map.64 = bf16[8,4,40,96]{3,2,1,0:T(8,128)(2,1)} custom-call(s32[6,32]{1,0:T(8,128)} %bitcast.9, bf16[32,40,96]{2,1,0:T(8,128)(2,1)} %bitcast.8, bf16[11,6,96,384]{3,2,1,0:T(8,128)(2,1)} %bitcast.6, s32[11,1280]{1,0:T(8,128)} %rows_ref.1, s32[11,1280]{1,0:T(8,128)} %cols_ref.1, f32[11,1280]{1,0:T(8,128)} %vals_ref.1), custom_call_target="tpu_custom_call" | custom-call | tf_op jit(solution)/shard_map/pallas_call | solution.py:234
  67.8 1.7 %copy.8 = bf16[32,96,40]{1,2,0:T(8,128)(2,1)} copy(bf16[32,96,40]{1,2,0:T(8,128)(2,1)} %bitcast.7) | data formatting | bytes 491520
